TPU v7x, 128 devices: a whole 4x4x4 slice. The times are simulated.
128 devices in a mesh: snap: 8 (over y_lo, z), rows: 16 (over y_hi, x, core).
Axes of the slice: x: 4, y: 4 (y_hi: 2, y_lo: 2; y = y_hi * 2 + y_lo), z: 4, core: 2. Of those that a mesh axis runs over, the one named last changes fastest.
Arguments:
- window_observations: bfloat16 [256, 2097152], P('snap', 'rows'), may hold values from -120 to 120
Outputs:
- transition_mapping: float32 [255, 255], replicated
- future_estimates: float32 [8, 2097152], P(None, ('rows', 'snap'))
All inputs are finite; a program needn't handle non-finite values.
Results may differ from a plain program's by a relative error of at most 0.0003.
Values may be sent and summed in bfloat16 or wider, within the bound.
A program may use at most 128 MiB of HBM per device.

v0:
```python
import jax
import jax.numpy as jnp
from jax import lax
from jax.sharding import PartitionSpec as P

H = 8


exact_arithmetic = lax.Precision.HIGHEST


def upper_factor(matrix):
    width = matrix.shape[0]
    positions = jnp.arange(width)

    def eliminate(col_index, state):
        working, lower = state
        column = lax.dynamic_slice_in_dim(working, col_index, 1, 1)[:, 0]
        pivot = jnp.sqrt(lax.dynamic_slice_in_dim(column, col_index, 1, 0)[0])
        scaled = jnp.where(positions >= col_index, column / pivot, jnp.float32(0.0))
        working = working - scaled[:, None] * scaled[None, :]
        lower = lax.dynamic_update_slice_in_dim(lower, scaled[:, None], col_index, 1)
        return (working, lower)

    start_state = (matrix, jnp.zeros((width, width), jnp.float32))
    return lax.fori_loop(0, width, eliminate, start_state)[1].T


def upper_inverse(upper):
    width = upper.shape[0]
    positions = jnp.arange(width)

    def substitute(step_index, inverse):
        row_index = width - 1 - step_index
        upper_row = lax.dynamic_slice_in_dim(upper, row_index, 1, 0)[0]
        pivot = lax.dynamic_slice_in_dim(upper_row, row_index, 1, 0)[0]
        unit_row = jnp.where(positions == row_index, jnp.float32(1.0), jnp.float32(0.0))
        new_row = (unit_row - jnp.dot(upper_row, inverse, precision=exact_arithmetic)) / pivot
        return lax.dynamic_update_slice_in_dim(inverse, new_row[None, :], row_index, 0)

    return lax.fori_loop(0, width, substitute, jnp.zeros((width, width), jnp.float32))


def per_device(window_observations):
    rowwise = lax.all_to_all(window_observations, "snap", split_axis=1, concat_axis=0, tiled=True)
    local_gram = jnp.dot(rowwise, rowwise.T, preferred_element_type=jnp.float32)
    upper_full = upper_factor(lax.psum(local_gram, ("snap", "rows")))
    principal_section = rowwise.shape[0] - 1
    upper_left_corner = upper_full[:principal_section, :principal_section]
    corner_inverse = upper_inverse(upper_left_corner)
    earlier = rowwise[:principal_section]
    basis_rows = jnp.dot(
        corner_inverse.T,
        earlier.astype(jnp.float32),
        precision=exact_arithmetic,
        preferred_element_type=jnp.float32,
    )
    later_rows = rowwise[1:].astype(jnp.float32)
    compressed_image = jnp.dot(
        basis_rows, later_rows.T, precision=exact_arithmetic, preferred_element_type=jnp.float32
    )
    coords = lax.psum(compressed_image, ("snap", "rows"))
    transition_mapping = jnp.dot(coords, corner_inverse, precision=exact_arithmetic)
    vector = coords[:, principal_section - 1]
    columns = []
    for horizon in range(H):
        vector = jnp.dot(transition_mapping, vector, precision=exact_arithmetic)
        columns.append(vector)
    stacked = jnp.stack(columns, axis=1)
    future_estimates = jnp.dot(
        stacked.T, basis_rows, precision=exact_arithmetic, preferred_element_type=jnp.float32
    )
    return (transition_mapping, future_estimates)


def solution(mesh):
    placed = (P("snap", "rows"),)
    return jax.shard_map(
        per_device,
        mesh=mesh,
        in_specs=placed,
        out_specs=(P(), P(None, ("rows", "snap"))),
        check_vma=False,
    )
```

profile of v0, /device:TPU:1, one launch (start us, length us, event | category | flops | bytes accessed | tf_op | source)
XLA Modules:
  0.0 1249.7 jit_solution(16025885766966775785)
XLA Ops:
  7.2 7.5 copy.11
  14.7 100.9 %all_to_all.19 = bf16[32,8,16384]{2,0,1:T(8,128)(2,1)S(1)} all-to-all(bf16[32,8,16384]{2,0,1:T(8,128)(2,1)} %bitcast.95), channel_id=1, replica_groups=mesh['snap'=8,'rows'=16] {'snap'}, dimensions={1} | all-to-all | bytes 16777216 | tf_op jit(solution)/shard_map/all_to_all | solution.py:45
  115.6 3.2 copy-done
  118.8 3.1 fusion.14
  122.2 142.3 %all-reduce.3.cloned.1.call-done = f32[256,256]{1,0:T(8,128)} async-done(((f32[256,256]{1,0:T(8,128)}), f32[256,256]{1,0:T(8,128)}) %all-reduce.3.cloned.1.call-update) | async-done | bytes 262160 | tf_op jit(solution)/shard_map/psum | solution.py:47
  264.5 1.1 copy.8
  265.6 387.9 %while.36 = (s32[]{:T(128)}, f32[256,256]{0,1:T(8,128)S(1)}, f32[256,256]{0,1:T(8,128)S(1)}, s32[]{:T(128)}, s32[]{:T(128)}, /*index=5*/s32[]{:T(128)}) while((s32[]{:T(128)}, f32[256,256]{0,1:T(8,128)S(1)}, f32[256,256]{0,1:T(8,128)S(1)}, s32[]{:T(128)}, s32[]{:T(128)}, /*index=5*/s32[]{:T(128)}) %tuple.89), condition=%wide.region_2.3_spmd.clone, body=%wide.region_1.2_spmd.clone.sunk | while | flops 132355 | bytes 534149 | solution.py:26
  653.5 394.7 %while.37 = (s32[]{:T(128)}, f32[255,255]{1,0:T(8,128)S(1)}, f32[255,255]{1,0:T(8,128)S(1)}, s32[]{:T(128)}, s32[]{:T(128)}, /*index=5*/s32[]{:T(128)}, s32[]{:T(128)}) while((s32[]{:T(128)}, f32[255,255]{1,0:T(8,128)S(1)}, f32[255,255]{1,0:T(8,128)S(1)}, s32[]{:T(128)}, s32[]{:T(128)}, /*index=5*/s32[]{:T(128)}, s32[]{:T(128)}) %tuple.99), condition=%wide.region_4.5_spmd.clone, body=%wide.region_3.4_spmd.clone.sunk | while | flops 781327 | bytes 268443 | solution.py:41
  654.3 0.7 fusion.49
  657.4 0.7 fusion.49
  659.0 0.7 fusion.49
  663.6 0.7 fusion.49
  665.2 0.7 fusion.49
  669.8 0.7 fusion.49
  671.3 0.7 fusion.49
  676.0 0.7 fusion.49
  677.5 0.7 fusion.49
  682.2 0.7 fusion.49
  1048.2 13.8 %fusion.12 = f32[255,16384]{1,0:T(8,128)} fusion(f32[255,255]{1,0:T(8,128)S(1)} %get-tuple-element.254, bf16[256,16384]{1,0:T(8,128)(2,1)} %bitcast.93), kind=kOutput, calls=%fused_computation.17 | convolution fusion | flops 12784435200 | bytes 25360388 | tf_op jit(solution)/shard_map/dot_general | solution.py:52
  1062.0 24.3 %fusion.10 = f32[255,255]{1,0:T(8,128)} fusion(f32[255,16384]{1,0:T(8,128)} %fusion.12, bf16[256,16384]{1,0:T(8,128)(2,1)} %bitcast.94), kind=kOutput, calls=%fused_computation.15 | convolution fusion | flops 12784435200 | bytes 25360388 | tf_op jit(solution)/shard_map/dot_general | solution.py:59
  1086.3 139.2 %all-reduce.5.cloned.1.call-done = f32[255,255]{1,0:T(8,128)} async-done(((f32[255,255]{1,0:T(8,128)}), f32[255,255]{1,0:T(8,128)}) %all-reduce.5.cloned.1.call-update) | async-done | bytes 260116 | tf_op jit(solution)/shard_map/psum | solution.py:62
  1225.5 1.3 fusion.15
  1226.8 1.2 slice_reduce_fusion
  1230.7 12.2 fusion.16
  (2564 shorter events, 578.0 us)
Async XLA Ops:
  7.2 257.3 %all-reduce.3.cloned.1.call-start = ((), (), s32[]{:S(2)}) async-start(), calls=%async_computation.1 | async-start | bytes 524288 | tf_op jit(solution)/shard_map/psum | solution.py:47
  115.6 3.2 copy-start
  121.9 1103.5 %all-reduce.5.cloned.1.call-start = ((), (), s32[]{:S(2)}) async-start(), calls=%async_computation.2 | async-start | bytes 524288 | tf_op jit(solution)/shard_map/psum | solution.py:62
  1226.8 16.0 %copy-start.1 = (f32[255,255]{1,0:T(8,128)}, f32[255,255]{1,0:T(8,128)S(1)}, u32[]{:S(2)}) copy-start(f32[255,255]{1,0:T(8,128)S(1)} %fusion.15) | copy-start | bytes 780304
Sparse Core Ops, SparseCore 0:
  122.1 142.3 all-reduce.2
  1086.4 138.9 all-reduce.4
where the time goes:
time: 1260 us; the launch traced here: 1250 us
  local copies, waits for them, and re-layouts  336 us (27%)
  waiting for transfers between devices  282 us (22%)
  other arithmetic  212 us (17%)
  loops' own time  201 us (16%)
  matrix products  104 us (8%)
  blocking collectives  101 us (8%)
  between operations  14.1 us (1%)
    another operation x1, loops' own time, upper_factor(): return lax.fori_loop(0, width, eliminate, start_state)[1].T  191 us
    div x255, other arithmetic, substitute(): (unit_row - jnp.dot(upper_row, inverse, precision=exact_arithmetic)) / pivot  177 us
    dynamic_slice x256, local copies, waits for them, and re-layouts, eliminate(): pivot = jnp.sqrt(lax.dynamic_slice_in_dim(column, col_index, 1, 0)[0])  151 us
    dynamic_slice x255, local copies, waits for them, and re-layouts, substitute(): pivot = lax.dynamic_slice_in_dim(upper_row, row_index, 1, 0)[0]  150 us
    psum x1, waiting for transfers between devices, per_device(): upper_full = upper_factor(lax.psum(local_gram, ('snap', 'rows')))  142 us
    psum x1, waiting for transfers between devices, per_device(): coords = lax.psum(compressed_image, ('snap', 'rows'))  139 us
    all_to_all x1, blocking collectives, per_device(): lax.all_to_all(window_observations, 'snap', split_axis=1, concat_axis=0,...  101 us
    dot_general x255, matrix products, substitute(): jnp.dot(upper_row, inverse, precision=exact_arithmetic)  46.7 us
  transfers between devices with their start and end apart: 2, of which 2 were waited for; matrix products, arithmetic and copies ran while one was open for 0% of the time, Pallas kernels for 0%

commit v1 on v0

v1 whole, which is shorter than its diff:
```python
import functools

import jax
import jax.numpy as jnp
from jax import lax
from jax.experimental import pallas as pl
from jax.experimental.pallas import tpu as pltpu
from jax.sharding import PartitionSpec as P

H = 8
BLOCK = 32
CHUNKS = 8
FORECAST_COLUMNS = 2048
MESH = pl.DeviceIdType.MESH
F32, BF16 = jnp.float32, jnp.bfloat16


def parts3(value):
    high = value.astype(BF16)
    rest = value - high.astype(F32)
    middle = rest.astype(BF16)
    low = (rest - middle.astype(F32)).astype(BF16)
    return high, middle, low


def exchange_kernel(n_snap, n_rows, x_ref, data_ref, gram_ref, held, total, slots, slab, laps,
                    own_sem, send_sem, recv_sem, out_sem, s1, r1, s2, r2, s3, r3):
    me_s, me_r = lax.axis_index("snap"), lax.axis_index("rows")
    block = x_ref.shape[0]
    states = data_ref.shape[1]
    width = states // CHUNKS
    share = gram_ref.shape[0] // n_rows

    def snap_peer(offset):
        return lax.rem(me_s + offset, n_snap)

    def rows_peer(offset):
        return lax.rem(me_r + offset, n_rows)

    barrier = pltpu.get_barrier_semaphore()
    for offset in range(1, n_snap):
        pl.semaphore_signal(barrier, inc=1, device_id=(snap_peer(offset), me_r), device_id_type=MESH)
    for offset in range(1, n_rows):
        pl.semaphore_signal(barrier, inc=1, device_id=(me_s, rows_peer(offset)), device_id_type=MESH)
    pl.semaphore_wait(barrier, n_snap + n_rows - 2)

    my_rows = pl.ds(pl.multiple_of(me_s * block, block), block)

    def columns(chunk):
        return pl.ds(pl.multiple_of(chunk * width, width), width)

    def own_copy(chunk):
        return pltpu.make_async_copy(
            x_ref.at[:, pl.ds(pl.multiple_of(me_s * states + chunk * width, width), width)],
            held.at[my_rows, columns(chunk)],
            own_sem.at[chunk],
        )

    def send(chunk, offset):
        peer = snap_peer(offset)
        return pltpu.make_async_remote_copy(
            src_ref=x_ref.at[:, pl.ds(pl.multiple_of(peer * states + chunk * width, width), width)],
            dst_ref=held.at[my_rows, columns(chunk)],
            send_sem=send_sem.at[chunk, offset],
            recv_sem=recv_sem.at[chunk, offset],
            device_id=(peer, me_r),
            device_id_type=MESH,
        )

    def start_chunk(chunk, carry):
        own_copy(chunk).start()
        for offset in range(1, n_snap):
            send(chunk, offset).start()
        return carry

    lax.fori_loop(0, CHUNKS, start_chunk, 0)
    total[...] = jnp.zeros_like(total)

    def out_copy(chunk):
        return pltpu.make_async_copy(held.at[:, columns(chunk)], data_ref.at[:, columns(chunk)], out_sem.at[chunk])

    def use_chunk(chunk, carry):
        own_copy(chunk).wait()
        for offset in range(1, n_snap):
            send(chunk, offset).wait_recv()
        out_copy(chunk).start()
        piece = held[:, columns(chunk)]
        total[...] += lax.dot_general(piece, piece, (((1,), (1,)), ((), ())), preferred_element_type=F32)
        return carry

    lax.fori_loop(0, CHUNKS, use_chunk, 0)

    def part_of(index):
        return pl.ds(pl.multiple_of(index * share, share), share)

    def first(offset):
        peer = rows_peer(offset)
        return pltpu.make_async_remote_copy(
            src_ref=total.at[part_of(peer)], dst_ref=slots.at[offset],
            send_sem=s1.at[offset], recv_sem=r1.at[offset],
            device_id=(me_s, peer), device_id_type=MESH,
        )

    for offset in range(1, n_rows):
        first(offset).start()
    mine = total[part_of(me_r)]
    for offset in range(1, n_rows):
        first(offset).wait_recv()
        mine = mine + slots[offset]
    slab[...] = mine

    def second(offset):
        return pltpu.make_async_remote_copy(
            src_ref=slab, dst_ref=laps.at[me_s],
            send_sem=s2.at[offset], recv_sem=r2.at[offset],
            device_id=(snap_peer(offset), me_r), device_id_type=MESH,
        )

    for offset in range(1, n_snap):
        second(offset).start()
    laps[me_s] = mine
    for offset in range(1, n_snap):
        second(offset).wait_recv()
    summed = laps[0]
    for index in range(1, n_snap):
        summed = summed + laps[index]
    gram_ref[part_of(me_r)] = summed

    def third(offset):
        return pltpu.make_async_remote_copy(
            src_ref=gram_ref.at[part_of(me_r)], dst_ref=gram_ref.at[part_of(me_r)],
            send_sem=s3.at[offset], recv_sem=r3.at[offset],
            device_id=(me_s, rows_peer(offset)), device_id_type=MESH,
        )

    for offset in range(1, n_rows):
        third(offset).start()
    for offset in range(1, n_rows):
        third(offset).wait_recv()
    for offset in range(1, n_rows):
        first(offset).wait_send()
        third(offset).wait_send()
    for offset in range(1, n_snap):
        second(offset).wait_send()

    def finish(chunk, carry):
        out_copy(chunk).wait()
        for offset in range(1, n_snap):
            send(chunk, offset).wait_send()
        return carry

    lax.fori_loop(0, CHUNKS, finish, 0)


def exchange(x, n_snap, n_rows):
    block, length = x.shape
    size, states = n_snap * block, length // n_snap
    share = size // n_rows
    dma = pltpu.SemaphoreType.DMA
    return pl.pallas_call(
        functools.partial(exchange_kernel, n_snap, n_rows),
        out_shape=(
            jax.ShapeDtypeStruct((size, states), BF16),
            jax.ShapeDtypeStruct((size, size), F32),
        ),
        in_specs=[pl.BlockSpec(memory_space=pltpu.HBM)],
        out_specs=(pl.BlockSpec(memory_space=pltpu.HBM), pl.BlockSpec(memory_space=pltpu.VMEM)),
        scratch_shapes=[
            pltpu.VMEM((size, states), BF16),
            pltpu.VMEM((size, size), F32),
            pltpu.VMEM((n_rows, share, size), F32),
            pltpu.VMEM((share, size), F32),
            pltpu.VMEM((n_snap, share, size), F32),
            dma((CHUNKS,)),
            dma((CHUNKS, n_snap)),
            dma((CHUNKS, n_snap)),
            dma((CHUNKS,)),
            dma((n_rows,)), dma((n_rows,)),
            dma((n_snap,)), dma((n_snap,)),
            dma((n_rows,)), dma((n_rows,)),
        ],
        compiler_params=pltpu.CompilerParams(
            collective_id=0, has_side_effects=True, vmem_limit_bytes=40 * 2**20
        ),
    )(x)


def factor_block(matrix):
    n = matrix.shape[0]
    rows = lax.broadcasted_iota(jnp.int32, (n, 128), 0)
    lanes = lax.broadcasted_iota(jnp.int32, (n, 128), 1)
    unit = jnp.where(lanes == rows + n, F32(1.0), F32(0.0))
    state = unit + jnp.concatenate([matrix, jnp.zeros((n, 128 - n), F32)], axis=1)
    for k in range(n - 1):
        column, row = state[:, k : k + 1], state[k : k + 1, :]
        inverse = F32(1.0) / state[k : k + 1, k : k + 1]
        state = state - (jnp.where(rows > k, column, F32(0.0)) * inverse) * row
    diagonal = jnp.sum(jnp.where(rows == lanes, state, F32(0.0)), axis=1, keepdims=True)
    return state, diagonal


def six_left(value, axis):
    high, middle, low = parts3(value)
    return jnp.concatenate([high, middle, high, low, high, middle], axis=axis)


def six_right(value, axis):
    high, middle, low = parts3(value)
    return jnp.concatenate([high, high, middle, high, low, middle], axis=axis)


def forecast_kernel(gram_ref, data_hbm, map_ref, future_ref, work, upper, lower, data, sems):
    size, states = data.shape
    pieces = sems.shape[0]
    width = states // pieces

    def fetch(index):
        part = pl.ds(index * width, width)
        return pltpu.make_async_copy(data_hbm.at[:, part], data.at[:, part], sems.at[index])

    for index in range(pieces):
        fetch(index).start()

    b = BLOCK
    work[...] = gram_ref[...]
    cols = lax.broadcasted_iota(jnp.int32, (b, size), 1)
    last = None
    for s in range(0, size, b):
        lines = work[s : s + b, :]
        state, diagonal = factor_block(lines[:, s : s + b])
        rows_b = lax.broadcasted_iota(jnp.int32, (b, size), 0)
        inside = (cols >= s) & (cols < s + b)
        lines = jnp.where(inside, jnp.where(cols == rows_b + s, F32(1.0), F32(0.0)), lines)
        solved = jnp.dot(
            six_left(state[:, b : 2 * b], 1), six_right(lines, 0), preferred_element_type=F32
        )
        if s + b < size:
            first = 0 if s + b < size // 2 else size // 2
            scaled = jnp.where(cols >= s + b, solved, F32(0.0)) * (F32(1.0) / diagonal)
            update = lax.dot_general(
                six_left(scaled[:, first:], 0), six_right(solved, 0), (((0,), (0,)), ((), ())),
                preferred_element_type=F32,
            )
            kept = work[s + b :, :]
            cols_k = lax.broadcasted_iota(jnp.int32, kept.shape, 1)
            kept = jnp.where((cols_k >= s) & (cols_k < s + b), F32(0.0), kept)
            work[s + b :, :] = kept - update[s + b - first :, :]
        root = lax.rsqrt(diagonal)
        corner = jnp.where(inside, F32(0.0), jnp.where(cols >= s + b, solved, F32(0.0)))
        placed = [state[:, :b]]
        if s:
            placed.insert(0, jnp.zeros((b, s), F32))
        if s + b < size:
            placed.append(jnp.zeros((b, size - s - b), F32))
        diag_rows = jnp.concatenate(placed, axis=1)
        diag_rows = jnp.where(cols >= rows_b + s, diag_rows, F32(0.0))
        upper[s : s + b, :] = (corner + diag_rows) * root
        low_rows = jnp.where(cols < s + b, solved, F32(0.0))
        lower[s : s + b, :] = low_rows * root
        last = low_rows

    cols_1 = lax.broadcasted_iota(jnp.int32, (1, size), 1)
    vector = jnp.where(cols_1 < size - 1, -last[b - 1 : b, :], F32(0.0))
    step, powers = vector, []
    for _ in range(H):
        moved = jnp.where((cols_1 >= 1) & (cols_1 < size - 1), pltpu.roll(step, 1, 1), F32(0.0))
        step = moved + vector * step[:, size - 2 : size - 1]
        powers.append(step)
    weights = jnp.concatenate(powers, axis=0)
    left = jnp.concatenate([part.astype(F32) for part in parts3(weights)], axis=0).astype(BF16)

    cols_w = lax.broadcasted_iota(jnp.int32, (size, size), 1)
    coords = jnp.where(cols_w < size - 1, pltpu.roll(upper[...], size - 1, 1), F32(0.0))
    mapping = lax.dot_general(
        coords, lower[...], (((1,), (1,)), ((), ())),
        precision=lax.Precision.HIGHEST, preferred_element_type=F32,
    )
    map_ref[...] = mapping[: size - 1, : size - 1]

    for index in range(pieces):
        fetch(index).wait()
        part = pl.ds(index * width, width)
        product = jnp.dot(left, data[:, part], preferred_element_type=F32)
        future_ref[:, part] = product[:H] + product[H : 2 * H] + product[2 * H :]


def forecast(gram, data):
    size, states = data.shape
    return pl.pallas_call(
        forecast_kernel,
        out_shape=(
            jax.ShapeDtypeStruct((size - 1, size - 1), F32),
            jax.ShapeDtypeStruct((H, states), F32),
        ),
        in_specs=[pl.BlockSpec(memory_space=pltpu.VMEM), pl.BlockSpec(memory_space=pltpu.HBM)],
        out_specs=(pl.BlockSpec(memory_space=pltpu.VMEM), pl.BlockSpec(memory_space=pltpu.VMEM)),
        scratch_shapes=[
            pltpu.VMEM((size, size), F32),
            pltpu.VMEM((size, size), F32),
            pltpu.VMEM((size, size), F32),
            pltpu.VMEM((size, states), BF16),
            pltpu.SemaphoreType.DMA((states // FORECAST_COLUMNS,)),
        ],
        compiler_params=pltpu.CompilerParams(vmem_limit_bytes=40 * 2**20),
    )(gram, data)


def solution(mesh):
    n_snap, n_rows = mesh.shape["snap"], mesh.shape["rows"]

    def per_device(window_observations):
        data, gram = exchange(window_observations, n_snap, n_rows)
        return forecast(gram, data)

    return jax.shard_map(
        per_device,
        mesh=mesh,
        in_specs=(P("snap", "rows"),),
        out_specs=(P(), P(None, ("rows", "snap"))),
        check_vma=False,
    )
```

time: 1260 us -> 166 us (0.13)
  local copies, waits for them, and re-layouts: 336 us -> 0 us
  waiting for transfers between devices: 282 us -> 0 us
  other arithmetic: 212 us -> 0 us
  loops' own time: 201 us -> 0 us
  Pallas kernels: 0 us -> 165 us
  matrix products: 104 us -> 0 us
  blocking collectives: 101 us -> 0 us
  between operations: 14.1 us -> 0.64 us
    dynamic_slice x511 -> x0, local copies, waits for them, and re-layouts: 301 us -> none  [the longest x256 151 us: eliminate(): pivot = jnp.sqrt(lax.dynamic_slice_in_dim(column, col_index, 1, 0)[0])]
    psum x2 -> x0, waiting for transfers between devices: 281 us -> none  [the longest x1 142 us: per_device(): upper_full = upper_factor(lax.psum(local_gram, ('snap', 'rows')))]
    another operation x2 -> x0, loops' own time: 201 us -> none  [the longest x1 191 us: upper_factor(): return lax.fori_loop(0, width, eliminate, start_state)[1].T]
    div x255 -> x0, other arithmetic: 177 us -> none  [substitute(): (unit_row - jnp.dot(upper_row, inverse, precision=exact_arithmetic)) / pivot]
    pallas_call x0 -> x2, Pallas kernels: none -> 165 us  [the longest x1 127 us: exchange(): pl.pallas_call(functools.partial(exchange_kernel, n_snap, n_rows), out_sh...]
    dot_general x268 -> x0, matrix products: 104 us -> none  [the longest x255 46.7 us: substitute(): jnp.dot(upper_row, inverse, precision=exact_arithmetic)]
    all_to_all x1 -> x0, blocking collectives: 101 us -> none  [per_device(): lax.all_to_all(window_observations, 'snap', split_axis=1, concat_axis=0,...]
    sub x256 -> x0, other arithmetic: 28.7 us -> none  [eliminate(): working = working - scaled[:, None] * scaled[None, :]]
  transfers between devices with their start and end apart: 2 -> 0, of which waited for: 2 -> 0; matrix products, arithmetic and copies ran while one was open for 0% -> 0% of each run, Pallas kernels for 0% -> 0%
where the time goes in v1:
time: 166 us
  Pallas kernels  165 us (99%)
    pallas_call x1, Pallas kernels, exchange(): pl.pallas_call(functools.partial(exchange_kernel, n_snap, n_rows), out_sh...  127 us
    pallas_call x1, Pallas kernels, forecast(): pl.pallas_call(forecast_kernel, out_shape=(jax.ShapeDtypeStruct((size - 1...  38 us

profile of v1, /device:TPU:1, one launch (start us, length us, event | category | flops | bytes accessed | tf_op | source)
XLA Modules:
  0.0 166.0 jit_solution(5940973292956308933)
XLA Ops:
  0.6 127.3 %shard_map.30 = (bf16[256,16384]{1,0:T(8,128)(2,1)S(1)}, f32[256,256]{1,0:T(8,128)S(1)}) custom-call(bf16[32,131072]{1,0:T(8,128)(2,1)} %x_ref.1), custom_call_target="tpu_custom_call" | custom-call | tf_op jit(solution)/shard_map/pallas_call | solution.py:160
  127.9 38.0 %shard_map.31 = (f32[255,255]{1,0:T(8,128)}, f32[8,16384]{1,0:T(8,128)}) custom-call(f32[256,256]{1,0:T(8,128)S(1)} %get-tuple-element.4.gram_ref, bf16[256,16384]{1,0:T(8,128)(2,1)S(1)} %get-tuple-element.5.data_hbm), custom_call_target="tpu_custom_call" | custom-call | tf_op jit(solution)/shard_map/pallas_call | solution.py:289

commit v2 on v1

--- a/solution.py
+++ b/solution.py
@@ -185,16 +185,51 @@
     )(x)
 
 
+def reciprocal(value):
+    guess = pltpu.reciprocal(value, approx=True)
+    for _ in range(2):
+        guess = guess * (F32(2.0) - value * guess)
+    return guess
+
+
 def factor_block(matrix):
     n = matrix.shape[0]
     rows = lax.broadcasted_iota(jnp.int32, (n, 128), 0)
     lanes = lax.broadcasted_iota(jnp.int32, (n, 128), 1)
     unit = jnp.where(lanes == rows + n, F32(1.0), F32(0.0))
-    state = unit + jnp.concatenate([matrix, jnp.zeros((n, 128 - n), F32)], axis=1)
-    for k in range(n - 1):
-        column, row = state[:, k : k + 1], state[k : k + 1, :]
-        inverse = F32(1.0) / state[k : k + 1, k : k + 1]
-        state = state - (jnp.where(rows > k, column, F32(0.0)) * inverse) * row
+    whole = unit + jnp.concatenate([matrix, jnp.zeros((n, 128 - n), F32)], axis=1)
+    eight = lax.broadcasted_iota(jnp.int32, (8, 128), 0)
+    tiles = [whole[k : k + 8] for k in range(0, n, 8)]
+
+    def spread(tile, lane):
+        return jnp.broadcast_to(tile[:, lane : lane + 1], (8, 128))
+
+    for now, tile in enumerate(tiles):
+        k = 8 * now
+        later = range(now + 1, len(tiles))
+        row = [jnp.broadcast_to(tile[i : i + 1], (8, 128)) for i in range(8)]
+        column = {t: [spread(tiles[t], k + i) for i in range(8)] for t in later}
+        pivot = [[spread(row[i], k + j) if j >= i else None for j in range(8)] for i in range(8)]
+        inverse = [None] * 8
+        for i in range(8):
+            if i == 7 and not later:
+                break
+            inverse[i] = reciprocal(pivot[i][i])
+            for j in range(i + 1, 8):
+                factor = pivot[i][j] * inverse[i]
+                for m in range(j, 8):
+                    pivot[j][m] = pivot[j][m] - factor * pivot[i][m]
+                row[j] = row[j] - factor * row[i]
+                for t in later:
+                    column[t][j] = column[t][j] - column[t][i] * factor
+        for t in later:
+            for i in range(8):
+                tiles[t] = tiles[t] - (column[t][i] * inverse[i]) * row[i]
+        done = row[0]
+        for i in range(1, 8):
+            done = jnp.where(eight == i, row[i], done)
+        tiles[now] = done
+    state = jnp.concatenate(tiles, axis=0)
     diagonal = jnp.sum(jnp.where(rows == lanes, state, F32(0.0)), axis=1, keepdims=True)
     return state, diagonal
 

time: 166 us -> 144 us (0.87)
  Pallas kernels: 165 us -> 143 us
    pallas_call x1, Pallas kernels: 38 us -> 16.1 us  [forecast(): pl.pallas_call(forecast_kernel, out_shape=(jax.ShapeDtypeStruct((size - 1...]
where the time goes in v2:
time: 144 us
  Pallas kernels  143 us (99%)
    pallas_call x1, Pallas kernels, exchange(): pl.pallas_call(functools.partial(exchange_kernel, n_snap, n_rows), out_sh...  127 us
    pallas_call x1, Pallas kernels, forecast(): pl.pallas_call(forecast_kernel, out_shape=(jax.ShapeDtypeStruct((size - 1...  16.1 us

profile of v2, /device:TPU:1, one launch (start us, length us, event | category | flops | bytes accessed | tf_op | source)
XLA Modules:
  0.0 144.1 jit_solution(2835319746094634614)
XLA Ops:
  0.6 127.3 %shard_map.30 = (bf16[256,16384]{1,0:T(8,128)(2,1)S(1)}, f32[256,256]{1,0:T(8,128)S(1)}) custom-call(bf16[32,131072]{1,0:T(8,128)(2,1)} %x_ref.1), custom_call_target="tpu_custom_call" | custom-call | tf_op jit(solution)/shard_map/pallas_call | solution.py:160
  127.9 16.1 %shard_map.31 = (f32[255,255]{1,0:T(8,128)}, f32[8,16384]{1,0:T(8,128)}) custom-call(f32[256,256]{1,0:T(8,128)S(1)} %get-tuple-element.4.gram_ref, bf16[256,16384]{1,0:T(8,128)(2,1)S(1)} %get-tuple-element.5.data_hbm), custom_call_target="tpu_custom_call" | custom-call | tf_op jit(solution)/shard_map/pallas_call | solution.py:324

commit v3 on v2

--- a/solution.py
+++ b/solution.py
@@ -10,6 +10,8 @@
 H = 8
 BLOCK = 32
 CHUNKS = 8
+EARLY = 3
+SIDE = 4
 FORECAST_COLUMNS = 2048
 MESH = pl.DeviceIdType.MESH
 F32, BF16 = jnp.float32, jnp.bfloat16
@@ -23,26 +25,29 @@
     return high, middle, low
 
 
-def exchange_kernel(n_snap, n_rows, x_ref, data_ref, gram_ref, held, total, slots, slab, laps,
-                    own_sem, send_sem, recv_sem, out_sem, s1, r1, s2, r2, s3, r3):
+def exchange_kernel(x_ref, data_ref, gram_ref, held, total, pair, quarters, slab, laps,
+                    near_sem, own_sem, send_sem, recv_sem, out_sem, sum_send, sum_recv):
     me_s, me_r = lax.axis_index("snap"), lax.axis_index("rows")
+    y_lo, z = me_s // SIDE, lax.rem(me_s, SIDE)
+    y_hi, x, core = me_r // (2 * SIDE), lax.rem(me_r // 2, SIDE), lax.rem(me_r, 2)
+    y = 2 * y_hi + y_lo
     block = x_ref.shape[0]
     states = data_ref.shape[1]
     width = states // CHUNKS
-    share = gram_ref.shape[0] // n_rows
-
-    def snap_peer(offset):
-        return lax.rem(me_s + offset, n_snap)
-
-    def rows_peer(offset):
-        return lax.rem(me_r + offset, n_rows)
-
-    barrier = pltpu.get_barrier_semaphore()
-    for offset in range(1, n_snap):
-        pl.semaphore_signal(barrier, inc=1, device_id=(snap_peer(offset), me_r), device_id_type=MESH)
-    for offset in range(1, n_rows):
-        pl.semaphore_signal(barrier, inc=1, device_id=(me_s, rows_peer(offset)), device_id_type=MESH)
-    pl.semaphore_wait(barrier, n_snap + n_rows - 2)
+
+    def device(dx=0, dy=0, dz=0, dc=0):
+        far_y = lax.rem(y + dy, SIDE)
+        far_x, far_z, far_c = lax.rem(x + dx, SIDE), lax.rem(z + dz, SIDE), lax.rem(core + dc, 2)
+        return (lax.rem(far_y, 2) * SIDE + far_z, (far_y // 2) * 2 * SIDE + far_x * 2 + far_c)
+
+    neighbours = [
+        device(dc=1), device(dx=1), device(dx=3), device(dy=1), device(dy=3), device(dz=1), device(dz=3)
+    ]
+
+    def greet(semaphore):
+        for neighbour in neighbours:
+            pl.semaphore_signal(semaphore, inc=1, device_id=neighbour, device_id_type=MESH)
+        pl.semaphore_wait(semaphore, len(neighbours))
 
     my_rows = pl.ds(pl.multiple_of(me_s * block, block), block)
 
@@ -57,7 +62,8 @@
         )
 
     def send(chunk, offset):
-        peer = snap_peer(offset)
+        dy, dz = offset // SIDE, offset % SIDE
+        peer = lax.rem(y_lo + dy, 2) * SIDE + lax.rem(z + dz, SIDE)
         return pltpu.make_async_remote_copy(
             src_ref=x_ref.at[:, pl.ds(pl.multiple_of(peer * states + chunk * width, width), width)],
             dst_ref=held.at[my_rows, columns(chunk)],
@@ -67,13 +73,30 @@
             device_id_type=MESH,
         )
 
-    def start_chunk(chunk, carry):
+    others = range(1, 2 * SIDE)
+
+    def start_chunks(first, last, offsets):
+        def start(chunk, carry):
+            for offset in offsets:
+                send(chunk, offset).start()
+            return carry
+
+        lax.fori_loop(first, last, start, 0)
+
+    greet(pltpu.get_barrier_semaphore())
+    start_chunks(0, EARLY, (4, 1, 3))
+    greet(near_sem.at[0])
+    start_chunks(0, EARLY, (2, 5, 7))
+    greet(near_sem.at[1])
+    start_chunks(0, EARLY, (6,))
+    start_chunks(EARLY, CHUNKS, (6, 5, 7, 2, 4, 1, 3))
+    greet(near_sem.at[2])
+
+    def start_own(chunk, carry):
         own_copy(chunk).start()
-        for offset in range(1, n_snap):
-            send(chunk, offset).start()
         return carry
 
-    lax.fori_loop(0, CHUNKS, start_chunk, 0)
+    lax.fori_loop(0, CHUNKS, start_own, 0)
     total[...] = jnp.zeros_like(total)
 
     def out_copy(chunk):
@@ -81,103 +104,114 @@
 
     def use_chunk(chunk, carry):
         own_copy(chunk).wait()
-        for offset in range(1, n_snap):
+        for offset in others:
             send(chunk, offset).wait_recv()
         out_copy(chunk).start()
         piece = held[:, columns(chunk)]
-        total[...] += lax.dot_general(piece, piece, (((1,), (1,)), ((), ())), preferred_element_type=F32)
+        half = piece.shape[0] // 2
+        dims = (((1,), (1,)), ((), ()))
+        top = lax.dot_general(piece[:half], piece, dims, preferred_element_type=F32)
+        total[:half] += top[:, :half]
+        total[half : 2 * half] += top[:, half:]
+        total[2 * half :] += lax.dot_general(piece[half:], piece[half:], dims, preferred_element_type=F32)
         return carry
 
     lax.fori_loop(0, CHUNKS, use_chunk, 0)
 
-    def part_of(index):
-        return pl.ds(pl.multiple_of(index * share, share), share)
-
-    def first(offset):
-        peer = rows_peer(offset)
-        return pltpu.make_async_remote_copy(
-            src_ref=total.at[part_of(peer)], dst_ref=slots.at[offset],
-            send_sem=s1.at[offset], recv_sem=r1.at[offset],
-            device_id=(me_s, peer), device_id_type=MESH,
+    height = total.shape[0]
+    half, share = height // 2, height // (2 * SIDE)
+    started = []
+
+    def move(source, target, where):
+        index = len(started)
+        copy = pltpu.make_async_remote_copy(
+            src_ref=source, dst_ref=target, send_sem=sum_send.at[index], recv_sem=sum_recv.at[index],
+            device_id=where, device_id_type=MESH,
         )
-
-    for offset in range(1, n_rows):
-        first(offset).start()
-    mine = total[part_of(me_r)]
-    for offset in range(1, n_rows):
-        first(offset).wait_recv()
-        mine = mine + slots[offset]
+        copy.start()
+        started.append(copy)
+        return copy
+
+    def half_of(index):
+        return pl.ds(pl.multiple_of(index * half, half), half)
+
+    def share_of(far_x):
+        return pl.ds(pl.multiple_of(core * half + far_x * share, share), share)
+
+    move(total.at[half_of(1 - core)], pair, device(dc=1)).wait_recv()
+    pair[...] = pair[...] + total[half_of(core)]
+
+    copies = []
+    for dx in (2, 1, 3):
+        part = pl.ds(pl.multiple_of(lax.rem(x + dx, SIDE) * share, share), share)
+        copies.append(move(pair.at[part], quarters.at[dx], device(dx=dx)))
+    mine = pair[pl.ds(pl.multiple_of(x * share, share), share)]
+    for dx, copy in zip((2, 1, 3), copies):
+        copy.wait_recv()
+        mine = mine + quarters[dx]
     slab[...] = mine
 
-    def second(offset):
-        return pltpu.make_async_remote_copy(
-            src_ref=slab, dst_ref=laps.at[me_s],
-            send_sem=s2.at[offset], recv_sem=r2.at[offset],
-            device_id=(snap_peer(offset), me_r), device_id_type=MESH,
-        )
-
-    for offset in range(1, n_snap):
-        second(offset).start()
-    laps[me_s] = mine
-    for offset in range(1, n_snap):
-        second(offset).wait_recv()
+    place = y * SIDE + z
+    copies = []
+    for dy in (2, 1, 3, 0):
+        for dz in (2, 1, 3, 0):
+            if dy or dz:
+                copies.append(move(slab, laps.at[place], device(dy=dy, dz=dz)))
+    laps[place] = mine
+    for copy in copies:
+        copy.wait_recv()
     summed = laps[0]
-    for index in range(1, n_snap):
+    for index in range(1, SIDE * SIDE):
         summed = summed + laps[index]
-    gram_ref[part_of(me_r)] = summed
-
-    def third(offset):
-        return pltpu.make_async_remote_copy(
-            src_ref=gram_ref.at[part_of(me_r)], dst_ref=gram_ref.at[part_of(me_r)],
-            send_sem=s3.at[offset], recv_sem=r3.at[offset],
-            device_id=(me_s, rows_peer(offset)), device_id_type=MESH,
-        )
-
-    for offset in range(1, n_rows):
-        third(offset).start()
-    for offset in range(1, n_rows):
-        third(offset).wait_recv()
-    for offset in range(1, n_rows):
-        first(offset).wait_send()
-        third(offset).wait_send()
-    for offset in range(1, n_snap):
-        second(offset).wait_send()
+    gram_ref[share_of(x)] = summed
+
+    copies = []
+    for dx in (2, 1, 3):
+        copies.append(move(gram_ref.at[share_of(x)], gram_ref.at[share_of(x)], device(dx=dx)))
+    for copy in copies:
+        copy.wait_recv()
+    move(gram_ref.at[half_of(core)], gram_ref.at[half_of(core)], device(dc=1)).wait_recv()
+    for copy in started:
+        copy.wait_send()
 
     def finish(chunk, carry):
         out_copy(chunk).wait()
-        for offset in range(1, n_snap):
+        for offset in others:
             send(chunk, offset).wait_send()
         return carry
 
     lax.fori_loop(0, CHUNKS, finish, 0)
 
 
-def exchange(x, n_snap, n_rows):
+def exchange(x):
     block, length = x.shape
-    size, states = n_snap * block, length // n_snap
-    share = size // n_rows
+    size, states = 2 * SIDE * block, length // (2 * SIDE)
+    height, lanes = 3 * size // 2, size // 2
+    share = height // (2 * SIDE)
     dma = pltpu.SemaphoreType.DMA
+    moves = 2 + 2 * (SIDE - 1) + SIDE * SIDE - 1
     return pl.pallas_call(
-        functools.partial(exchange_kernel, n_snap, n_rows),
+        exchange_kernel,
         out_shape=(
             jax.ShapeDtypeStruct((size, states), BF16),
-            jax.ShapeDtypeStruct((size, size), F32),
+            jax.ShapeDtypeStruct((height, lanes), F32),
         ),
         in_specs=[pl.BlockSpec(memory_space=pltpu.HBM)],
         out_specs=(pl.BlockSpec(memory_space=pltpu.HBM), pl.BlockSpec(memory_space=pltpu.VMEM)),
         scratch_shapes=[
             pltpu.VMEM((size, states), BF16),
-            pltpu.VMEM((size, size), F32),
-            pltpu.VMEM((n_rows, share, size), F32),
-            pltpu.VMEM((share, size), F32),
-            pltpu.VMEM((n_snap, share, size), F32),
+            pltpu.VMEM((height, lanes), F32),
+            pltpu.VMEM((height // 2, lanes), F32),
+            pltpu.VMEM((SIDE, share, lanes), F32),
+            pltpu.VMEM((share, lanes), F32),
+            pltpu.VMEM((SIDE * SIDE, share, lanes), F32),
+            pltpu.SemaphoreType.REGULAR((3,)),
             dma((CHUNKS,)),
-            dma((CHUNKS, n_snap)),
-            dma((CHUNKS, n_snap)),
+            dma((CHUNKS, 2 * SIDE)),
+            dma((CHUNKS, 2 * SIDE)),
             dma((CHUNKS,)),
-            dma((n_rows,)), dma((n_rows,)),
-            dma((n_snap,)), dma((n_snap,)),
-            dma((n_rows,)), dma((n_rows,)),
+            dma((moves,)),
+            dma((moves,)),
         ],
         compiler_params=pltpu.CompilerParams(
             collective_id=0, has_side_effects=True, vmem_limit_bytes=40 * 2**20
@@ -257,7 +291,11 @@
         fetch(index).start()
 
     b = BLOCK
-    work[...] = gram_ref[...]
+    half = size // 2
+    work[:half, :half] = gram_ref[:half]
+    work[:half, half:] = gram_ref[half : 2 * half]
+    work[half:, half:] = gram_ref[2 * half :]
+    work[half:, :half] = jnp.zeros((half, half), F32)
     cols = lax.broadcasted_iota(jnp.int32, (b, size), 1)
     last = None
     for s in range(0, size, b):
@@ -341,10 +379,8 @@
 
 
 def solution(mesh):
-    n_snap, n_rows = mesh.shape["snap"], mesh.shape["rows"]
-
     def per_device(window_observations):
-        data, gram = exchange(window_observations, n_snap, n_rows)
+        data, gram = exchange(window_observations)
         return forecast(gram, data)
 
     return jax.shard_map(

time: 144 us -> 135 us (0.938)
  Pallas kernels: 143 us -> 134 us
    pallas_call x1, Pallas kernels: 127 us -> 118 us  [exchange(): pl.pallas_call(exchange_kernel, out_shape=(jax.ShapeDtypeStruct((size, st...]
where the time goes in v3:
time: 135 us
  Pallas kernels  134 us (99%)
    pallas_call x1, Pallas kernels, exchange(): pl.pallas_call(exchange_kernel, out_shape=(jax.ShapeDtypeStruct((size, st...  118 us
    pallas_call x1, Pallas kernels, forecast(): pl.pallas_call(forecast_kernel, out_shape=(jax.ShapeDtypeStruct((size - 1...  16.1 us

profile of v3, /device:TPU:1, one launch (start us, length us, event | category | flops | bytes accessed | tf_op | source)
XLA Modules:
  0.0 134.9 jit_solution(14166896383937725723)
XLA Ops:
  0.6 118.1 %shard_map.30 = (bf16[256,16384]{1,0:T(8,128)(2,1)S(1)}, f32[384,128]{1,0:T(8,128)S(1)}) custom-call(bf16[32,131072]{1,0:T(8,128)(2,1)} %x_ref.1), custom_call_target="tpu_custom_call" | custom-call | tf_op jit(solution)/shard_map/pallas_call | solution.py:193
  118.7 16.1 %shard_map.31 = (f32[255,255]{1,0:T(8,128)}, f32[8,16384]{1,0:T(8,128)}) custom-call(f32[384,128]{1,0:T(8,128)S(1)} %get-tuple-element.4.gram_ref, bf16[256,16384]{1,0:T(8,128)(2,1)S(1)} %get-tuple-element.5.data_hbm), custom_call_target="tpu_custom_call" | custom-call | tf_op jit(solution)/shard_map/pallas_call | solution.py:362

commit v4 on v3

--- a/solution.py
+++ b/solution.py
@@ -138,17 +138,15 @@
     def share_of(far_x):
         return pl.ds(pl.multiple_of(core * half + far_x * share, share), share)
 
-    move(total.at[half_of(1 - core)], pair, device(dc=1)).wait_recv()
-    pair[...] = pair[...] + total[half_of(core)]
-
+    eight = [(dx, dc) for dx in (2, 1, 3) for dc in (0, 1)] + [(0, 1)]
     copies = []
-    for dx in (2, 1, 3):
-        part = pl.ds(pl.multiple_of(lax.rem(x + dx, SIDE) * share, share), share)
-        copies.append(move(pair.at[part], quarters.at[dx], device(dx=dx)))
-    mine = pair[pl.ds(pl.multiple_of(x * share, share), share)]
-    for dx, copy in zip((2, 1, 3), copies):
+    for slot, (dx, dc) in enumerate(eight):
+        part = pl.ds(pl.multiple_of(lax.rem(core + dc, 2) * half + lax.rem(x + dx, SIDE) * share, share), share)
+        copies.append(move(total.at[part], pair.at[slot], device(dx=dx, dc=dc)))
+    mine = total[share_of(x)]
+    for slot, copy in reversed(list(enumerate(copies))):
         copy.wait_recv()
-        mine = mine + quarters[dx]
+        mine = mine + pair[slot]
     slab[...] = mine
 
     place = y * SIDE + z
@@ -166,11 +164,10 @@
     gram_ref[share_of(x)] = summed
 
     copies = []
-    for dx in (2, 1, 3):
-        copies.append(move(gram_ref.at[share_of(x)], gram_ref.at[share_of(x)], device(dx=dx)))
+    for dx, dc in eight:
+        copies.append(move(gram_ref.at[share_of(x)], gram_ref.at[share_of(x)], device(dx=dx, dc=dc)))
     for copy in copies:
         copy.wait_recv()
-    move(gram_ref.at[half_of(core)], gram_ref.at[half_of(core)], device(dc=1)).wait_recv()
     for copy in started:
         copy.wait_send()
 
@@ -189,7 +186,7 @@
     height, lanes = 3 * size // 2, size // 2
     share = height // (2 * SIDE)
     dma = pltpu.SemaphoreType.DMA
-    moves = 2 + 2 * (SIDE - 1) + SIDE * SIDE - 1
+    moves = 14 + SIDE * SIDE - 1
     return pl.pallas_call(
         exchange_kernel,
         out_shape=(
@@ -201,7 +198,7 @@
         scratch_shapes=[
             pltpu.VMEM((size, states), BF16),
             pltpu.VMEM((height, lanes), F32),
-            pltpu.VMEM((height // 2, lanes), F32),
+            pltpu.VMEM((7, share, lanes), F32),
             pltpu.VMEM((SIDE, share, lanes), F32),
             pltpu.VMEM((share, lanes), F32),
             pltpu.VMEM((SIDE * SIDE, share, lanes), F32),
@@ -219,18 +216,11 @@
     )(x)
 
 
-def reciprocal(value):
-    guess = pltpu.reciprocal(value, approx=True)
-    for _ in range(2):
-        guess = guess * (F32(2.0) - value * guess)
-    return guess
-
-
 def factor_block(matrix):
     n = matrix.shape[0]
     rows = lax.broadcasted_iota(jnp.int32, (n, 128), 0)
     lanes = lax.broadcasted_iota(jnp.int32, (n, 128), 1)
-    unit = jnp.where(lanes == rows + n, F32(1.0), F32(0.0))
+    unit = jnp.where((lanes >= n) & (lax.rem(lanes, n) == rows), F32(1.0), F32(0.0))
     whole = unit + jnp.concatenate([matrix, jnp.zeros((n, 128 - n), F32)], axis=1)
     eight = lax.broadcasted_iota(jnp.int32, (8, 128), 0)
     tiles = [whole[k : k + 8] for k in range(0, n, 8)]
@@ -242,17 +232,24 @@
         k = 8 * now
         later = range(now + 1, len(tiles))
         row = [jnp.broadcast_to(tile[i : i + 1], (8, 128)) for i in range(8)]
+        pivot = [[spread(row[i], k + j) if j >= i else None for j in range(8)] for i in range(8)]
         column = {t: [spread(tiles[t], k + i) for i in range(8)] for t in later}
-        pivot = [[spread(row[i], k + j) if j >= i else None for j in range(8)] for i in range(8)]
         inverse = [None] * 8
+        scale = None
         for i in range(8):
             if i == 7 and not later:
                 break
-            inverse[i] = reciprocal(pivot[i][i])
+            near = pltpu.reciprocal(pivot[i][i], approx=True)
+            off = pivot[i][i] * near
+            exact = near * (F32(2.0) - off)
+            exact = exact * (F32(2.0) - pivot[i][i] * exact)
+            inverse[i] = exact if scale is None else exact * scale
+            scale = off if scale is None else scale * off
             for j in range(i + 1, 8):
-                factor = pivot[i][j] * inverse[i]
+                factor = pivot[i][j] * exact
+                rough = pivot[i][j] * near
                 for m in range(j, 8):
-                    pivot[j][m] = pivot[j][m] - factor * pivot[i][m]
+                    pivot[j][m] = off * pivot[j][m] - rough * pivot[i][m]
                 row[j] = row[j] - factor * row[i]
                 for t in later:
                     column[t][j] = column[t][j] - column[t][i] * factor
@@ -266,6 +263,18 @@
     state = jnp.concatenate(tiles, axis=0)
     diagonal = jnp.sum(jnp.where(rows == lanes, state, F32(0.0)), axis=1, keepdims=True)
     return state, diagonal
+
+
+def solve(state, lines):
+    n = state.shape[0]
+    lanes = lax.broadcasted_iota(jnp.int32, state.shape, 1)
+    high, middle, low = [part.astype(F32) for part in parts3(state)]
+    second = jnp.where(lanes < 3 * n, middle, low)
+    left = jnp.concatenate([high, second], axis=1).astype(BF16)
+    high, middle, low = parts3(lines)
+    none = jnp.zeros_like(high)
+    right = jnp.concatenate([none, high, middle, low, none, high, middle, high], axis=0)
+    return jnp.dot(left, right, preferred_element_type=F32)
 
 
 def six_left(value, axis):
@@ -304,9 +313,7 @@
         rows_b = lax.broadcasted_iota(jnp.int32, (b, size), 0)
         inside = (cols >= s) & (cols < s + b)
         lines = jnp.where(inside, jnp.where(cols == rows_b + s, F32(1.0), F32(0.0)), lines)
-        solved = jnp.dot(
-            six_left(state[:, b : 2 * b], 1), six_right(lines, 0), preferred_element_type=F32
-        )
+        solved = solve(state, lines)
         if s + b < size:
             first = 0 if s + b < size // 2 else size // 2
             scaled = jnp.where(cols >= s + b, solved, F32(0.0)) * (F32(1.0) / diagonal)

time: 135 us -> 132 us (0.978)
  Pallas kernels: 134 us -> 132 us
    pallas_call x1, Pallas kernels: 16.1 us -> 14.5 us  [forecast(): pl.pallas_call(forecast_kernel, out_shape=(jax.ShapeDtypeStruct((size - 1...]
where the time goes in v4:
time: 132 us
  Pallas kernels  132 us (100%)
    pallas_call x1, Pallas kernels, exchange(): pl.pallas_call(exchange_kernel, out_shape=(jax.ShapeDtypeStruct((size, st...  117 us
    pallas_call x1, Pallas kernels, forecast(): pl.pallas_call(forecast_kernel, out_shape=(jax.ShapeDtypeStruct((size - 1...  14.5 us

profile of v4, /device:TPU:1, one launch (start us, length us, event | category | flops | bytes accessed | tf_op | source)
XLA Modules:
  0.0 132.4 jit_solution(7814215108585189120)
XLA Ops:
  0.6 117.3 %shard_map.30 = (bf16[256,16384]{1,0:T(8,128)(2,1)S(1)}, f32[384,128]{1,0:T(8,128)S(1)}) custom-call(bf16[32,131072]{1,0:T(8,128)(2,1)} %x_ref.1), custom_call_target="tpu_custom_call" | custom-call | tf_op jit(solution)/shard_map/pallas_call | solution.py:190
  117.9 14.5 %shard_map.31 = (f32[255,255]{1,0:T(8,128)}, f32[8,16384]{1,0:T(8,128)}) custom-call(f32[384,128]{1,0:T(8,128)S(1)} %get-tuple-element.4.gram_ref, bf16[256,16384]{1,0:T(8,128)(2,1)S(1)} %get-tuple-element.5.data_hbm), custom_call_target="tpu_custom_call" | custom-call | tf_op jit(solution)/shard_map/pallas_call | solution.py:369

commit v5 on v4

--- a/solution.py
+++ b/solution.py
@@ -25,7 +25,7 @@
     return high, middle, low
 
 
-def exchange_kernel(x_ref, data_ref, gram_ref, held, total, pair, quarters, slab, laps,
+def exchange_kernel(x_ref, data_ref, gram_ref, held, total, packed, pair, slab, laps,
                     near_sem, own_sem, send_sem, recv_sem, out_sem, sum_send, sum_recv):
     me_s, me_r = lax.axis_index("snap"), lax.axis_index("rows")
     y_lo, z = me_s // SIDE, lax.rem(me_s, SIDE)
@@ -118,7 +118,14 @@
 
     lax.fori_loop(0, CHUNKS, use_chunk, 0)
 
-    height = total.shape[0]
+    height = packed.shape[0]
+    quarter = height // 5
+    packed[:quarter] = total[:quarter]
+    packed[quarter : 4 * quarter] = total[2 * quarter : 5 * quarter]
+    side = lax.broadcasted_iota(jnp.int32, (quarter, 2 * quarter), 1)
+    packed[4 * quarter :] = jnp.where(
+        side < quarter, pltpu.roll(total[5 * quarter :], quarter, 1), total[quarter : 2 * quarter]
+    )
     half, share = height // 2, height // (2 * SIDE)
     started = []
 
@@ -142,8 +149,8 @@
     copies = []
     for slot, (dx, dc) in enumerate(eight):
         part = pl.ds(pl.multiple_of(lax.rem(core + dc, 2) * half + lax.rem(x + dx, SIDE) * share, share), share)
-        copies.append(move(total.at[part], pair.at[slot], device(dx=dx, dc=dc)))
-    mine = total[share_of(x)]
+        copies.append(move(packed.at[part], pair.at[slot], device(dx=dx, dc=dc)))
+    mine = packed[share_of(x)]
     for slot, copy in reversed(list(enumerate(copies))):
         copy.wait_recv()
         mine = mine + pair[slot]
@@ -156,6 +163,17 @@
             if dy or dz:
                 copies.append(move(slab, laps.at[place], device(dy=dy, dz=dz)))
     laps[place] = mine
+
+    def finish(chunk, carry):
+        out_copy(chunk).wait()
+        for offset in others:
+            send(chunk, offset).wait_send()
+        return carry
+
+    lax.fori_loop(0, CHUNKS, finish, 0)
+
+    for copy in started[:7]:
+        copy.wait_send()
     for copy in copies:
         copy.wait_recv()
     summed = laps[0]
@@ -166,24 +184,18 @@
     copies = []
     for dx, dc in eight:
         copies.append(move(gram_ref.at[share_of(x)], gram_ref.at[share_of(x)], device(dx=dx, dc=dc)))
+    for copy in started[7 : len(started) - 7]:
+        copy.wait_send()
     for copy in copies:
         copy.wait_recv()
-    for copy in started:
+    for copy in copies:
         copy.wait_send()
-
-    def finish(chunk, carry):
-        out_copy(chunk).wait()
-        for offset in others:
-            send(chunk, offset).wait_send()
-        return carry
-
-    lax.fori_loop(0, CHUNKS, finish, 0)
 
 
 def exchange(x):
     block, length = x.shape
     size, states = 2 * SIDE * block, length // (2 * SIDE)
-    height, lanes = 3 * size // 2, size // 2
+    height, lanes = 5 * size // 4, size // 2
     share = height // (2 * SIDE)
     dma = pltpu.SemaphoreType.DMA
     moves = 14 + SIDE * SIDE - 1
@@ -197,9 +209,9 @@
         out_specs=(pl.BlockSpec(memory_space=pltpu.HBM), pl.BlockSpec(memory_space=pltpu.VMEM)),
         scratch_shapes=[
             pltpu.VMEM((size, states), BF16),
+            pltpu.VMEM((3 * lanes, lanes), F32),
             pltpu.VMEM((height, lanes), F32),
             pltpu.VMEM((7, share, lanes), F32),
-            pltpu.VMEM((SIDE, share, lanes), F32),
             pltpu.VMEM((share, lanes), F32),
             pltpu.VMEM((SIDE * SIDE, share, lanes), F32),
             pltpu.SemaphoreType.REGULAR((3,)),
@@ -301,9 +313,12 @@
 
     b = BLOCK
     half = size // 2
-    work[:half, :half] = gram_ref[:half]
-    work[:half, half:] = gram_ref[half : 2 * half]
-    work[half:, half:] = gram_ref[2 * half :]
+    quarter = half // 2
+    work[:quarter, :half] = gram_ref[:quarter]
+    work[:half, half:] = gram_ref[quarter : 3 * quarter]
+    work[half : half + quarter, half:] = gram_ref[3 * quarter : 4 * quarter]
+    work[quarter:half, :half] = gram_ref[4 * quarter :]
+    work[half + quarter :, half:] = pltpu.roll(gram_ref[4 * quarter :], quarter, 1)
     work[half:, :half] = jnp.zeros((half, half), F32)
     cols = lax.broadcasted_iota(jnp.int32, (b, size), 1)
     last = None

time: 132 us -> 132 us (level)
  no operation moved by 1% of the time
where the time goes in v5:
time: 132 us
  Pallas kernels  131 us (99%)
    pallas_call x1, Pallas kernels, exchange(): pl.pallas_call(exchange_kernel, out_shape=(jax.ShapeDtypeStruct((size, st...  116 us
    pallas_call x1, Pallas kernels, forecast(): pl.pallas_call(forecast_kernel, out_shape=(jax.ShapeDtypeStruct((size - 1...  14.7 us

profile of v5, /device:TPU:1, one launch (start us, length us, event | category | flops | bytes accessed | tf_op | source)
XLA Modules:
  0.0 131.7 jit_solution(5806824205830236414)
XLA Ops:
  0.6 116.3 %shard_map.30 = (bf16[256,16384]{1,0:T(8,128)(2,1)S(1)}, f32[320,128]{1,0:T(8,128)S(1)}) custom-call(bf16[32,131072]{1,0:T(8,128)(2,1)} %x_ref.1), custom_call_target="tpu_custom_call" | custom-call | tf_op jit(solution)/shard_map/pallas_call | solution.py:202
  116.9 14.7 %shard_map.31 = (f32[255,255]{1,0:T(8,128)}, f32[8,16384]{1,0:T(8,128)}) custom-call(f32[320,128]{1,0:T(8,128)S(1)} %get-tuple-element.4.gram_ref, bf16[256,16384]{1,0:T(8,128)(2,1)S(1)} %get-tuple-element.5.data_hbm), custom_call_target="tpu_custom_call" | custom-call | tf_op jit(solution)/shard_map/pallas_call | solution.py:384

commit v6 on v5

--- a/solution.py
+++ b/solution.py
@@ -12,7 +12,7 @@
 CHUNKS = 8
 EARLY = 3
 SIDE = 4
-FORECAST_COLUMNS = 2048
+FORECAST_COLUMNS = 8192
 MESH = pl.DeviceIdType.MESH
 F32, BF16 = jnp.float32, jnp.bfloat16
 

time: 132 us -> 131 us (level)
  no operation moved by 1% of the time
where the time goes in v6:
time: 131 us
  Pallas kernels  130 us (99%)
    pallas_call x1, Pallas kernels, exchange(): pl.pallas_call(exchange_kernel, out_shape=(jax.ShapeDtypeStruct((size, st...  116 us
    pallas_call x1, Pallas kernels, forecast(): pl.pallas_call(forecast_kernel, out_shape=(jax.ShapeDtypeStruct((size - 1...  13.9 us

profile of v6, /device:TPU:1, one launch (start us, length us, event | category | flops | bytes accessed | tf_op | source)
XLA Modules:
  0.0 130.9 jit_solution(613203531579858269)
XLA Ops:
  0.6 116.3 %shard_map.30 = (bf16[256,16384]{1,0:T(8,128)(2,1)S(1)}, f32[320,128]{1,0:T(8,128)S(1)}) custom-call(bf16[32,131072]{1,0:T(8,128)(2,1)} %x_ref.1), custom_call_target="tpu_custom_call" | custom-call | tf_op jit(solution)/shard_map/pallas_call | solution.py:202
  116.9 13.9 %shard_map.31 = (f32[255,255]{1,0:T(8,128)}, f32[8,16384]{1,0:T(8,128)}) custom-call(f32[320,128]{1,0:T(8,128)S(1)} %get-tuple-element.4.gram_ref, bf16[256,16384]{1,0:T(8,128)(2,1)S(1)} %get-tuple-element.5.data_hbm), custom_call_target="tpu_custom_call" | custom-call | tf_op jit(solution)/shard_map/pallas_call | solution.py:384
